TPU v7x, 256 devices: a whole 4x4x8 slice. The times are simulated.
256 devices in a mesh: tm: 32 (over z, y), state: 8 (over x, core).
Axes of the slice: x: 4, y: 4, z: 8, core: 2. Of those that a mesh axis runs over, the one named last changes fastest.
Arguments:
- observations: bfloat16 [512, 256, 384], P('tm', 'state'), may hold values from -6 to 6
- mask: int32 [512], P('tm'), may hold values 0 or 1
- transition: float32 [512, 512], P(None, 'state'), may hold values from -1 to 1
- updated_transition: float32 [512, 512], P(None, 'state'), may hold values from -1 to 1
- smoother_gain: float32 [512, 512], P(None, 'state'), may hold values from -1 to 1
- obs_gain: float32 [512, 384], replicated, may hold values from -0.02734375 to 0.02734375
- initial_mean: float32 [256, 512], P('state'), may hold values from -6 to 6
Outputs:
- filtered: float32 [512, 256, 512], P('tm', 'state')
- smoothed: float32 [512, 256, 512], P('tm', 'state')
All inputs are finite; a program needn't handle non-finite values. No bound on the sum of `mask` on one device may be relied on, other than what follows from the above.
Results may differ from a plain program's by a relative error of at most 0.0003.
Values sent between devices are 32-bit elements; how exact they have to be, the bound alone decides.
No kernel may reach another device: no remote copies, remote signals or barrier semaphores. Data moves between devices by JAX's collectives and lax.ppermute only.
A program may use at most 256 MiB of HBM per device.

v0:
```python
import jax
import jax.numpy as jnp
from jax import lax
from jax.sharding import PartitionSpec as P


def prefix(part, axis, combine, identity, reverse):
    count = lax.axis_size(axis)
    place = lax.axis_index(axis)
    ahead = count - 1 - place if reverse else place
    gathered = jax.tree.map(lambda a: lax.all_gather(a, axis), part)
    state = jax.tree.map(lambda a, e: jnp.zeros_like(a) + jnp.asarray(e, a.dtype), part, identity)

    def one(step, state):
        source = count - 1 - step if reverse else step
        return combine(
            state, jax.tree.map(lambda a: lax.dynamic_index_in_dim(a, source, 0, False), gathered)
        )

    return lax.fori_loop(0, ahead, one, state)


def times_transpose(left, right):
    return lax.dot_general(
        left,
        right,
        (((1,), (1,)), ((), ())),
        precision=lax.Precision.HIGHEST,
        preferred_element_type=jnp.float32,
    )


def matmul(left, right):
    return jnp.dot(left, right, precision=lax.Precision.HIGHEST, preferred_element_type=jnp.float32)


def widen(columns):
    return lax.all_gather(columns, "state", axis=1, tiled=True)


def compose(earlier, later):
    return (matmul(later[0], earlier[0]), times_transpose(earlier[1], later[0]) + later[1])


def local(
    observations, mask, transition, updated_transition, smoother_gain, obs_gain, initial_mean
):
    full_f, full_fo, full_g = (
        lax.all_gather(transition, "state", axis=1, tiled=True),
        lax.all_gather(updated_transition, "state", axis=1, tiled=True),
        lax.all_gather(smoother_gain, "state", axis=1, tiled=True),
    )
    panel = transition.shape[1]
    width = full_f.shape[0]
    steps = observations.shape[0]
    trials = observations.shape[1]
    count = lax.axis_size("tm")
    position = lax.axis_index("tm")
    first = position == 0
    final = position == count - 1
    identity = jnp.eye(width, dtype=jnp.float32)
    start_col = lax.axis_index("state") * panel
    own_cols = lax.dynamic_slice_in_dim(identity, start_col, panel, 1)
    flags = mask.astype(jnp.float32)
    frames = observations.astype(jnp.float32).reshape(steps * trials, observations.shape[2])
    drive = times_transpose(frames, obs_gain).reshape(steps, trials, width) * flags[:, None, None]

    def run_forward(start):

        def advance(mean, inputs):
            frame_drive, flag = inputs
            chosen = jnp.where(flag > 0, full_fo, full_f)
            mean = times_transpose(mean, chosen) + frame_drive
            return (mean, mean)

        return lax.scan(advance, start, (drive, mask))[1]

    def grow_forward(columns, flag):
        chosen = jnp.where(flag > 0, full_fo, full_f)
        return (matmul(chosen, columns), None)

    fwd_cols = lax.scan(grow_forward, own_cols, mask)[0]
    fwd_matrix = jnp.where(first, jnp.zeros_like(identity), widen(fwd_cols))
    zeros = jnp.zeros_like(initial_mean)
    fwd_local = run_forward(jnp.where(first, initial_mean, zeros))[-1]
    fwd_in = prefix((fwd_matrix, fwd_local), "tm", compose, (identity, zeros), False)[1]
    filtered = run_forward(jnp.where(first, initial_mean, fwd_in))
    virtual = times_transpose(filtered[-1], full_f)
    flat = filtered.reshape(steps * trials, width)
    gaps = (flat - times_transpose(times_transpose(flat, full_f), full_g)).reshape(
        steps, trials, width
    )

    def run_backward(start):

        def retreat(later, gap):
            value = times_transpose(later, full_g) + gap
            return (value, value)

        return lax.scan(retreat, start, gaps, reverse=True)[1]

    def grow_backward(turn, columns):
        return matmul(full_g, columns)

    back_cols = lax.fori_loop(0, steps, grow_backward, own_cols)
    back_matrix = jnp.where(final, jnp.zeros_like(identity), widen(back_cols))
    back_local = run_backward(jnp.where(final, virtual, zeros))[0]
    back_in = prefix((back_matrix, back_local), "tm", compose, (identity, zeros), True)[1]
    smoothed = run_backward(jnp.where(final, virtual, back_in))
    return (filtered, smoothed)


def solution(mesh):
    placed = (
        P("tm", "state", None),
        P("tm"),
        P(None, "state"),
        P(None, "state"),
        P(None, "state"),
        P(),
        P("state", None),
    )
    return jax.shard_map(
        local,
        mesh=mesh,
        in_specs=placed,
        out_specs=(P("tm", "state", None), P("tm", "state", None)),
        check_vma=False,
    )
```

profile of v0, /device:TPU:2, one launch (start us, length us, event | category | flops | bytes accessed | tf_op | source)
XLA Modules:
  0.0 917.4 jit_solution(580879077761360670)
XLA Ops:
  9.5 27.6 %all-gather.12.cloned.1.call-done = f32[512,512]{0,1:T(8,128)} async-done(((f32[512,64]{0,1:T(8,128)}), f32[512,512]{0,1:T(8,128)}) %all-gather.12.cloned.1.call-update) | async-done | bytes 1048592 | tf_op jit(solution)/shard_map/all_gather | solution.py:50
  38.7 26.1 %all-gather.14.cloned.1.call-done = f32[512,512]{0,1:T(8,128)} async-done(((f32[512,64]{0,1:T(8,128)}), f32[512,512]{0,1:T(8,128)}) %all-gather.14.cloned.1.call-update) | async-done | bytes 1048592 | tf_op jit(solution)/shard_map/all_gather | solution.py:49
  66.3 49.6 %while.102 = (s32[]{:T(128)}, f32[512,64]{0,1:T(8,128)S(1)}, s32[16]{0:T(128)}, f32[512,512]{1,0:T(8,128)S(1)}, f32[512,512]{1,0:T(8,128)S(1)}, /*index=5*/s32[]{:T(128)}, s32[1]{0:T(128)}) while((s32[]{:T(128)}, f32[512,64]{0,1:T(8,128)S(1)}, s32[16]{0:T(128)}, f32[512,512]{1,0:T(8,128)S(1)}, f32[512,512]{1,0:T(8,128)S(1)}, ...), condition=%wide.region_1.2_spmd, body=%wide.region_0.1_spmd.sunk | while | flops 201588736 | bytes 2621547 | solution.py:82
  118.6 18.7 %while.106 = (s32[]{:T(128)}, f32[512,64]{0,1:T(8,128)S(1)}, f32[512,512]{1,0:T(8,128)S(1)}, s32[]{:T(128)}) while((s32[]{:T(128)}, f32[512,64]{0,1:T(8,128)S(1)}, f32[512,512]{1,0:T(8,128)S(1)}, s32[]{:T(128)}) %tuple.192), condition=%wide.region_9.10_spmd, body=%wide.region_8.9_spmd.sunk | while | flops 201326592 | bytes 1572917 | solution.py:105
  138.0 4.7 all-gather.16.cloned.1.call-done
  145.4 3.0 convolution_multiply_fusion
  149.5 72.1 %while.103 = (s32[]{:T(128)}, f32[32,512]{1,0:T(8,128)S(1)}, f32[16,32,512]{2,1,0:T(8,128)}, s32[16]{0:T(128)}, f32[512,512]{1,0:T(8,128)S(1)}, /*index=5*/f32[5...) while((s32[]{:T(128)}, f32[32,512]{1,0:T(8,128)S(1)}, f32[16,32,512]{2,1,0:T(8,128)}, ...), condition=%wide.region_3.4_spmd, body=%wide.region_2.3_spmd.sunk | while | flops 100941824 | bytes 2491006 | solution.py:76
  151.4 3.0 bitcast_dynamic-update-slice_fusion.8
  156.2 2.6 bitcast_dynamic-update-slice_fusion.8
  187.0 2.6 bitcast_dynamic-update-slice_fusion.8
  200.2 3.0 bitcast_dynamic-update-slice_fusion.8
  205.1 3.0 bitcast_dynamic-update-slice_fusion.8
  218.7 3.0 bitcast_dynamic-update-slice_fusion.8
  225.7 182.3 %all-gather.26.cloned.1.call-done = f32[16384,512]{0,1:T(8,128)} async-done(((f32[512,512]{0,1:T(8,128)}), f32[16384,512]{0,1:T(8,128)}) %all-gather.26.cloned.1.call-update) | async-done | bytes 33554448 | tf_op jit(solution)/shard_map/all_gather | solution.py:11
  408.0 33.5 %copy.25 = f32[16384,512]{1,0:T(8,128)} copy(f32[16384,512]{0,1:T(8,128)} %all-gather.26.cloned.1.call-done) | data formatting | bytes 67108864 | tf_op jit(solution)/shard_map/while | solution.py:20
  441.5 44.1 %all-gather.18.cloned.1.call-done = f32[32,32,512]{2,1,0:T(8,128)} async-done(((f32[1,32,512]{2,1,0:T(8,128)}), f32[32,32,512]{2,1,0:T(8,128)}) %all-gather.18.cloned.1.call-update) | async-done | bytes 2097168 | tf_op jit(solution)/shard_map/all_gather | solution.py:11
  486.8 62.8 %while.105 = (s32[]{:T(128)}, f32[32,512]{1,0:T(8,128)S(1)}, f32[16,32,512]{2,1,0:T(8,128)}, s32[16]{0:T(128)S(1)}, f32[512,512]{1,0:T(8,128)S(1)}, /*index=5*/f...) while((s32[]{:T(128)}, f32[32,512]{1,0:T(8,128)S(1)}, f32[16,32,512]{2,1,0:T(8,128)}, ...), condition=%wide.region_7.8_spmd, body=%wide.region_6.7_spmd.sunk | while | flops 100941824 | bytes 2491006 | solution.py:76
  488.0 3.0 bitcast_dynamic-update-slice_fusion.9
  499.9 2.6 bitcast_dynamic-update-slice_fusion.9
  507.6 2.6 bitcast_dynamic-update-slice_fusion.9
  526.7 2.6 bitcast_dynamic-update-slice_fusion.9
  530.5 3.0 bitcast_dynamic-update-slice_fusion.9
  534.8 3.0 bitcast_dynamic-update-slice_fusion.9
  546.6 3.0 bitcast_dynamic-update-slice_fusion.9
  551.6 3.4 fusion.23
  555.0 4.7 convolution_subtract_fusion
  559.8 30.9 %while.107 = (s32[]{:T(128)}, f32[32,512]{1,0:T(8,128)S(1)}, f32[16,32,512]{2,1,0:T(8,128)S(1)}, f32[512,512]{1,0:T(8,128)S(1)}, f32[16,32,512]{2,1,0:T(8,128)}, /*index=5*/s32[]{:T(128)}, s32[]{:T(128)}) while((s32[]{:T(128)}, f32[32,512]{1,0:T(8,128)S(1)}, f32[16,32,512]{2,1,0:T(8,128)S(1)}, f32[512,512]{1,0:T(8,128)S(1)}, ...), condition=%wide.region_11.12_spmd, body=%wide.region_10.11_spmd.sunk | while | flops 100679680 | bytes 1441893 | solution.py:100
  591.3 127.4 %all-gather.28.cloned.1.call-done = f32[16384,512]{0,1:T(8,128)} async-done(((f32[512,512]{0,1:T(8,128)}), f32[16384,512]{0,1:T(8,128)}) %all-gather.28.cloned.1.call-update) | async-done | bytes 33554448 | tf_op jit(solution)/shard_map/all_gather | solution.py:11
  718.8 33.5 %copy.22 = f32[16384,512]{1,0:T(8,128)} copy(f32[16384,512]{0,1:T(8,128)} %all-gather.28.cloned.1.call-done) | data formatting | bytes 67108864 | tf_op jit(solution)/shard_map/all_gather | solution.py:11
  752.3 44.7 %all-gather.24.cloned.1.call-done = f32[32,32,512]{2,1,0:T(8,128)} async-done(((f32[1,32,512]{2,1,0:T(8,128)}), f32[32,32,512]{2,1,0:T(8,128)}) %all-gather.24.cloned.1.call-update) | async-done | bytes 2097168 | tf_op jit(solution)/shard_map/all_gather | solution.py:11
  797.0 72.4 %while.108 = (s32[]{:T(128)}, f32[32,512]{1,0:T(8,128)S(1)}, s32[]{:T(128)}, f32[32,512,512]{2,1,0:T(8,128)}, f32[32,32,512]{2,1,0:T(8,128)}, /*index=5*/s32[]{:T(128)}, s32[]{:T(128)}, s32[]{:T(128)}, s32[]{:T(128)}) while((s32[]{:T(128)}, f32[32,512]{1,0:T(8,128)S(1)}, s32[]{:T(128)}, f32[32,512,512]{2,1,0:T(8,128)}, ...), condition=%wide.region_13.14_spmd, body=%wide.region_12.13_spmd.sunk | while | flops 100679688 | bytes 1377427 | solution.py:20
  870.5 40.4 %while.109 = (s32[]{:T(128)}, f32[32,512]{1,0:T(8,128)S(1)}, f32[16,32,512]{2,1,0:T(8,128)}, f32[512,512]{1,0:T(8,128)S(1)}, f32[16,32,512]{2,1,0:T(8,128)}, /*index=5*/s32[]{:T(128)}, s32[]{:T(128)}) while((s32[]{:T(128)}, f32[32,512]{1,0:T(8,128)S(1)}, f32[16,32,512]{2,1,0:T(8,128)}, f32[512,512]{1,0:T(8,128)S(1)}, ...), condition=%wide.region_15.16_spmd, body=%wide.region_14.15_spmd.sunk | while | flops 100679680 | bytes 1441893 | solution.py:100
  (344 shorter events, 299.2 us)
Async XLA Ops:
  7.2 138.2 %copy-start = (f32[512,384]{1,0:T(8,128)S(1)}, f32[512,384]{1,0:T(8,128)}, u32[]{:S(2)}) copy-start(f32[512,384]{1,0:T(8,128)} %param.28) | copy-start | bytes 2359300
  7.2 29.9 %all-gather.12.cloned.1.call-start = ((), (), s32[]{:S(2)}) async-start(), calls=%async_computation | async-start | bytes 1179648 | tf_op jit(solution)/shard_map/all_gather | solution.py:50
  7.9 56.9 %all-gather.14.cloned.1.call-start = ((), (), s32[]{:S(2)}) async-start(), calls=%async_computation.1 | async-start | bytes 1179648 | tf_op jit(solution)/shard_map/all_gather | solution.py:49
  8.7 108.3 %all-gather.20.cloned.1.call-start = ((), (), s32[]{:S(2)}) async-start(), calls=%async_computation.4 | async-start | bytes 1179648 | tf_op jit(solution)/shard_map/all_gather | solution.py:51
  9.4 133.4 %all-gather.16.cloned.1.call-start = ((), (), s32[]{:S(2)}) async-start(), calls=%async_computation.2 | async-start | bytes 1179648 | tf_op jit(solution)/shard_map/all_gather | solution.py:38
  116.0 0.7 copy-start.3
  116.0 1.0 copy-start.2
  116.7 106.6 %all-gather.22.cloned.1.call-start = ((), (), s32[]{:S(2)}) async-start(), calls=%async_computation.5 | async-start | bytes 1179648 | tf_op jit(solution)/shard_map/all_gather | solution.py:38
  137.3 0.6 copy-start.4
  138.0 270.1 %all-gather.26.cloned.1.call-start = ((), (), s32[]{:S(2)}) async-start(), calls=%async_computation.7 | async-start | bytes 34603008 | tf_op jit(solution)/shard_map/all_gather | solution.py:11
  143.9 341.8 %all-gather.18.cloned.1.call-start = ((), (), s32[]{:S(2)}) async-start(), calls=%async_computation.3 | async-start | bytes 2162688 | tf_op jit(solution)/shard_map/all_gather | solution.py:11
  223.2 495.6 %all-gather.28.cloned.1.call-start = ((), (), s32[]{:S(2)}) async-start(), calls=%async_computation.8 | async-start | bytes 34603008 | tf_op jit(solution)/shard_map/all_gather | solution.py:11
  225.6 571.4 %all-gather.24.cloned.1.call-start = ((), (), s32[]{:S(2)}) async-start(), calls=%async_computation.6 | async-start | bytes 2162688 | tf_op jit(solution)/shard_map/all_gather | solution.py:11
  225.7 260.0 %copy-start.5 = (f32[32,512]{1,0:T(8,128)S(1)}, f32[32,512]{1,0:T(8,128)}, u32[]{:S(2)}) copy-start(f32[32,512]{1,0:T(8,128)} %param.29) | copy-start | bytes 196612
  225.7 261.1 %copy-start.6 = (s32[16]{0:T(128)S(1)}, s32[16]{0:T(128)}, u32[]{:S(2)}) copy-start(s32[16]{0:T(128)} %get-tuple-element.1101) | copy-start | bytes 196
  591.3 319.5 %copy-start.1 = (f32[512,384]{1,0:T(8,128)S(1)}, f32[512,384]{1,0:T(8,128)}, u32[]{:S(2)}) copy-start(f32[512,384]{1,0:T(8,128)} %param.28) | copy-start | bytes 2359300
Sparse Core Ops, SparseCore 0:
  9.9 27.1 all-gather.11
  39.0 25.7 all-gather.13
  66.6 25.8 all-gather.19
  116.8 25.9 all-gather.15
  144.5 25.6 all-gather.21
  173.1 234.8 all-gather.25
  410.6 74.9 all-gather.17
  488.2 230.4 all-gather.27
  721.9 74.9 all-gather.23
where the time goes:
time: 923 us; the launch traced here: 917 us
  waiting for transfers between devices  459 us (50%)
  matrix products  277 us (30%)
  local copies, waits for them, and re-layouts  129 us (14%)
  loops' own time  32.3 us (3%)
  between operations  14 us (2%)
    all_gather x4, waiting for transfers between devices, prefix(): gathered = jax.tree.map(lambda a: lax.all_gather(a, axis), part)  399 us
    dot_general x99, matrix products, times_transpose(): lax.dot_general(left, right, (((1,), (1,)), ((), ())), precision=lax.Prec...  241 us
    dynamic_slice x48, local copies, waits for them, and re-layouts, local(): fwd_cols = lax.scan(grow_forward, own_cols, mask)[0]  49.4 us
    dot_general x32, matrix products, matmul(): jnp.dot(left, right, precision=lax.Precision.HIGHEST, preferred_element_t...  36.9 us
    all_gather x1, local copies, waits for them, and re-layouts, prefix(): gathered = jax.tree.map(lambda a: lax.all_gather(a, axis), part)  33.5 us
    while x1, local copies, waits for them, and re-layouts, prefix(): return lax.fori_loop(0, ahead, one, state)  33.5 us
    all_gather x1, waiting for transfers between devices, local(): lax.all_gather(updated_transition, 'state', axis=1, tiled=True)  27.6 us
    all_gather x1, waiting for transfers between devices, local(): lax.all_gather(transition, 'state', axis=1, tiled=True)  26.1 us
  transfers between devices with their start and end apart: 9, of which 7 were waited for; matrix products, arithmetic and copies ran while one was open for 32% of the time, Pallas kernels for 0%

commit v1 on v0

v1 whole, which is shorter than its diff:
```python
import functools

import jax
import jax.numpy as jnp
from jax import lax
from jax.experimental import pallas as pl
from jax.experimental.pallas import tpu as pltpu
from jax.sharding import PartitionSpec as P

F32 = jnp.float32
BF16 = jnp.bfloat16
VMEM = pl.BlockSpec(memory_space=pltpu.VMEM)
SMEM = pl.BlockSpec(memory_space=pltpu.SMEM)
LIMIT = 50 * 1024 * 1024


def split(a):
    high = a.astype(BF16)
    return high, (a - high.astype(F32)).astype(BF16)


def dot(left, right):
    return jnp.dot(left, right, preferred_element_type=F32)


def dot3(a, high, low):
    rows = a.shape[0]
    a_high, a_low = split(a)
    both = dot(jnp.concatenate([a_high, a_low], 0), high)
    return both[:rows] + both[rows:] + dot(a_high, low)


def call(kernel, outs, specs, args, name, flops, scratch=()):
    return pl.pallas_call(
        kernel,
        out_shape=outs,
        in_specs=specs,
        out_specs=jax.tree.map(lambda _: VMEM, outs),
        scratch_shapes=list(scratch),
        compiler_params=pltpu.CompilerParams(vmem_limit_bytes=LIMIT),
        cost_estimate=pl.CostEstimate(flops=flops, bytes_accessed=4 << 20, transcendentals=0),
        name=name,
    )(*args)


def shape(*dims, dtype=F32):
    return jax.ShapeDtypeStruct(dims, dtype)


def drive_kernel(mask_ref, frames_ref, gain_ref, out_ref):
    high, low = split(gain_ref[...])
    frames = frames_ref[...]
    turned = (((1,), (1,)), ((), ()))
    drive = lax.dot_general(frames, high, turned, preferred_element_type=F32)
    drive = drive + lax.dot_general(frames, low, turned, preferred_element_type=F32)
    steps, trials, _ = out_ref.shape
    for t in range(steps):
        out_ref[t] = drive[t * trials : (t + 1) * trials] * mask_ref[t].astype(F32)


def local_kernel(place_ref, mask_ref, *refs):
    pieces, (drive_ref, start_ref, last_ref, high_ref, low_ref) = refs[:8], refs[8:]
    panel, width = pieces[0].shape[1:]
    for i, piece in enumerate(pieces):
        row = pl.multiple_of(place_ref[i] * panel, panel)
        across = lax.broadcasted_iota(jnp.int32, (panel, width), 1)
        down = lax.broadcasted_iota(jnp.int32, (panel, width), 0) + row
        eye = jnp.where(across == down, 1.0, 0.0).astype(F32)
        for m in range(2):
            high, low = split(piece[m] - eye)
            high_ref[m, pl.ds(row, panel), :] = high
            low_ref[m, pl.ds(row, panel), :] = low

    def step(t, mean):
        m = mask_ref[t]
        return mean + dot3(mean, high_ref[m], low_ref[m]) + drive_ref[t]

    last_ref[...] = lax.fori_loop(0, drive_ref.shape[0], step, start_ref[...])


def table_kernel(core_ref, pattern_ref, high_ref, low_ref, l1_ref, l2_ref, l3_ref, l4_ref, near_ref, v4_ref, v8_ref,
                 ph_ref, pl_ref, th_ref, tl_ref):
    width = high_ref.shape[1]

    def compose(eh, el, lh, ll):
        product = dot(eh, lh) + dot(el, lh) + dot(eh, ll)
        whole = eh.astype(F32) + el.astype(F32) + lh.astype(F32) + ll.astype(F32)
        return split(product + whole)

    def pair(i, _):
        first, second = lax.rem(i, 2), lax.div(i, 2)
        high, low = compose(high_ref[first], low_ref[first], high_ref[second], low_ref[second])
        ph_ref[i], pl_ref[i] = high, low
        return 0

    lax.fori_loop(0, 4, pair, 0)

    def quad(i, _):
        first, second = lax.rem(i, 4), lax.div(i, 4)
        high, low = compose(ph_ref[first], pl_ref[first], ph_ref[second], pl_ref[second])
        th_ref[i], tl_ref[i] = high, low
        return 0

    lax.fori_loop(0, 16, quad, 0)
    th_ref[16] = jnp.zeros((width, width), BF16)
    tl_ref[16] = jnp.zeros((width, width), BF16)

    quads = pattern_ref.shape[0]
    near = l4_ref[...]
    for block, later in enumerate((l3_ref, l2_ref, l1_ref)):

        def forward(i, mean, block=block):
            q = pattern_ref[quads - 12 + 4 * block + i]
            return mean + dot3(mean, th_ref[q], tl_ref[q])

        near = lax.fori_loop(0, 4, forward, near) + later[...]
    near_ref[...] = near

    half = v8_ref.shape[1]
    across = lax.broadcasted_iota(jnp.int32, (width, half), 1) + core_ref[0] * half
    down = lax.broadcasted_iota(jnp.int32, (width, half), 0)
    v8_ref[...] = jnp.where(across == down, 1.0, 0.0).astype(F32)

    def extend(i, _):
        q = pattern_ref[quads - 1 - i]
        high, low = split(v8_ref[...])
        v8_ref[...] += dot(th_ref[q], high) + dot(tl_ref[q], high) + dot(th_ref[q], low)
        return 0

    lax.fori_loop(0, 16, extend, 0)
    v4_ref[...] = v8_ref[...]
    lax.fori_loop(16, 32, extend, 0)


def powers_kernel(gain_ref, fh_ref, fl_ref, gh_ref, gl_ref, g4h_ref, g4l_ref, kh_ref, kl_ref, far_ref, now_ref):
    width = gain_ref.shape[0]
    across = lax.broadcasted_iota(jnp.int32, (width, width), 1)
    down = lax.broadcasted_iota(jnp.int32, (width, width), 0)
    now_ref[...] = gain_ref[...] - jnp.where(across == down, 1.0, 0.0).astype(F32)
    high, low = split(now_ref[...])
    gh_ref[...], gl_ref[...] = high, low
    product = dot(fh_ref[0], high) + dot(fl_ref[0], high) + dot(fh_ref[0], low)
    both = fh_ref[0].astype(F32) + fl_ref[0].astype(F32) + now_ref[...]
    kh_ref[...], kl_ref[...] = split(product + both)

    def square(i, _):
        high, low = split(now_ref[...])
        now_ref[...] = 2.0 * now_ref[...] + dot(high, high) + dot(low, high) + dot(high, low)

        @pl.when(i == 1)
        def _():
            g4h_ref[...], g4l_ref[...] = split(now_ref[...])

        @pl.when(i >= 3)
        def _():
            far_ref[i - 3] = now_ref[...]

        return 0

    lax.fori_loop(0, 8, square, 0)


def forward_kernel(mask_ref, final_ref, start_ref, drive_ref, bh_ref, bl_ref, gh_ref, gl_ref, g4h_ref, g4l_ref, kh_ref,
                   kl_ref, filtered_ref, gap_ref, part_ref, back_ref, virtual_ref):
    steps, trials, width = drive_ref.shape
    groups, inner = gap_ref.shape[:2]

    def step(t, mean):
        m = mask_ref[t]
        mean = mean + dot3(mean, bh_ref[m], bl_ref[m]) + drive_ref[t]
        filtered_ref[t] = mean
        return mean

    last = lax.fori_loop(0, steps, step, start_ref[...])
    virtual = last + dot3(last, bh_ref[0], bl_ref[0])
    virtual_ref[...] = virtual
    for g in range(groups):
        flat = filtered_ref[g * inner : (g + 1) * inner].reshape(inner * trials, width)
        gap_ref[g] = -dot3(flat, kh_ref[...], kl_ref[...]).reshape(inner, trials, width)
    value = gap_ref[:, inner - 1].reshape(groups * trials, width)
    for j in range(inner - 2, -1, -1):
        value = value + dot3(value, gh_ref[...], gl_ref[...]) + gap_ref[:, j].reshape(groups * trials, width)
    part = value.reshape(groups, trials, width)
    part_ref[...] = part
    carry = jnp.where(final_ref[0] > 0, virtual, jnp.zeros_like(virtual))
    for g in range(groups - 1, -1, -1):
        carry = carry + dot3(carry, g4h_ref[...], g4l_ref[...]) + part[g]
    back_ref[...] = carry


def backward_kernel(start_ref, gap_ref, part_ref, gh_ref, gl_ref, g4h_ref, g4l_ref, out_ref):
    groups, inner, trials, width = gap_ref.shape
    carry = start_ref[...]
    starts = [carry]
    for g in range(groups - 1, 0, -1):
        carry = carry + dot3(carry, g4h_ref[...], g4l_ref[...]) + part_ref[g]
        starts.insert(0, carry)
    value = jnp.concatenate(starts, 0)
    for j in range(inner - 1, -1, -1):
        value = value + dot3(value, gh_ref[...], gl_ref[...]) + gap_ref[:, j].reshape(groups * trials, width)
        out_ref[:, j] = value.reshape(groups, trials, width)


def high_dot(left, right):
    return jnp.dot(left, right, precision=lax.Precision.HIGH, preferred_element_type=F32)


def local(observations, mask, transition, updated_transition, smoother_gain, obs_gain, initial_mean):
    steps, trials, channels = observations.shape
    width, panel = transition.shape
    count = lax.axis_size("tm")
    chips = lax.axis_size("state") // 2
    block = lax.axis_index("tm")
    place = lax.axis_index("state")
    chip, core = place // 2, place % 2

    def along_x(a, k):
        return lax.ppermute(
            a, "state", [(2 * i + c, 2 * ((i + k) % chips) + c) for i in range(chips) for c in range(2)]
        )

    def swap(a):
        return lax.ppermute(a, "state", [(2 * i + c, 2 * i + 1 - c) for i in range(chips) for c in range(2)])

    def later(a, k):
        moved = lax.ppermute(a, "tm", [(i, (i + k) % count) for i in range(count)])
        return jnp.where(block >= k, moved, jnp.zeros_like(moved))

    own = jnp.stack([transition.T, updated_transition.T])
    mine = [own] + [along_x(own, k) for k in (1, 2, 3)]
    theirs = [swap(a) for a in mine]
    sources = jnp.stack([(chip - k) % chips for k in range(4)])
    places = jnp.concatenate([2 * sources + core, 2 * sources + 1 - core]).astype(jnp.int32)
    gain = lax.all_gather(smoother_gain.T, "state", axis=0, tiled=True)

    quads = steps // 4
    code = jnp.sum(mask.reshape(quads, 4) * jnp.array([1, 2, 4, 8], jnp.int32), axis=1)
    codes = lax.all_to_all(jnp.tile(code[None], (count, 1)), "tm", 0, 0, tiled=True).reshape(count * quads)
    padded = jnp.concatenate([jnp.full((8 * quads,), 16, jnp.int32), codes])
    patterns = lax.dynamic_slice_in_dim(padded, quads * block, 8 * quads, 0)

    drive = call(
        drive_kernel,
        shape(steps, trials, width),
        [SMEM, VMEM, VMEM],
        (mask, observations.reshape(steps * trials, channels), obs_gain),
        "drive",
        4 * steps * trials * channels * width,
    )

    square = width * width
    start = jnp.where(block == 0, initial_mean, jnp.zeros_like(initial_mean))
    last, bh, bl = call(
        local_kernel,
        (shape(trials, width), shape(2, width, width, dtype=BF16), shape(2, width, width, dtype=BF16)),
        [SMEM, SMEM] + [VMEM] * 10,
        (places, mask, *mine, *theirs, drive, start),
        "local",
        60 * trials * steps * square // 4,
    )
    before = [later(last, k) for k in (1, 2, 3, 4)]
    half = width // 2
    near, v4, v8 = call(
        table_kernel,
        (shape(trials, width), shape(width, half), shape(width, half)),
        [SMEM, SMEM] + [VMEM] * 6,
        (core.reshape(1).astype(jnp.int32), patterns, bh, bl, *before),
        "table",
        6 * 20 * square * width,
        (
            pltpu.VMEM((4, width, width), BF16),
            pltpu.VMEM((4, width, width), BF16),
            pltpu.VMEM((17, width, width), BF16),
            pltpu.VMEM((17, width, width), BF16),
        ),
    )
    v4_other, v8_other = swap(v4), swap(v8)

    def apply(mean, mine, theirs):
        here, there = high_dot(mean, mine), high_dot(mean, theirs)
        return jnp.where(
            core == 0, jnp.concatenate([here, there], 1), jnp.concatenate([there, here], 1)
        )

    mean = near + apply(later(near, 4), v4, v4_other)
    reach = mean
    for _ in range(3):
        mean = reach + apply(later(mean, 8), v8, v8_other)
    mean = jnp.where(block == 0, initial_mean, mean)

    bf = functools.partial(shape, width, width, dtype=BF16)
    gh, gl, g4h, g4l, kh, kl, far = call(
        powers_kernel,
        (bf(), bf(), bf(), bf(), bf(), bf(), shape(5, width, width)),
        [VMEM] * 3,
        (gain, bh, bl),
        "powers",
        6 * 9 * square * width,
        (pltpu.VMEM((width, width), F32),),
    )

    final = block == count - 1
    filtered, gap, part, back, virtual = call(
        forward_kernel,
        (
            shape(steps, trials, width),
            shape(4, steps // 4, trials, width),
            shape(4, trials, width),
            shape(trials, width),
            shape(trials, width),
        ),
        [SMEM, SMEM] + [VMEM] * 10,
        (mask, final.reshape(1).astype(jnp.int32), mean, drive, bh, bl, gh, gl, g4h, g4l, kh, kl),
        "forward",
        60 * trials * steps * square // 4,
    )

    scan = lax.all_to_all(back, "tm", 0, 0, tiled=True)
    for k in range(5):
        ahead = jnp.concatenate([scan[2**k :], jnp.zeros((2**k, width), F32)], 0)
        scan = scan + ahead + high_dot(ahead, far[k])
    ahead = jnp.concatenate([scan[1:], jnp.zeros((1, width), F32)], 0)
    back_in = lax.all_to_all(ahead, "tm", 0, 0, tiled=True)
    smoothed = call(
        backward_kernel,
        shape(4, steps // 4, trials, width),
        [VMEM] * 7,
        (jnp.where(final, virtual, back_in), gap, part, gh, gl, g4h, g4l),
        "backward",
        60 * trials * steps * square // 4,
    )
    return filtered, smoothed.reshape(steps, trials, width)


def solution(mesh):
    placed = (
        P("tm", "state", None),
        P("tm"),
        P(None, "state"),
        P(None, "state"),
        P(None, "state"),
        P(),
        P("state", None),
    )
    return jax.shard_map(
        local,
        mesh=mesh,
        in_specs=placed,
        out_specs=(P("tm", "state", None), P("tm", "state", None)),
        check_vma=False,
    )
```

time: 923 us -> 201 us (0.22)
  waiting for transfers between devices: 459 us -> 34 us
  matrix products: 277 us -> 4.04 us
  local copies, waits for them, and re-layouts: 129 us -> 7.87 us
  Pallas kernels: 0 us -> 81 us
  blocking collectives: 0 us -> 32.4 us
  loops' own time: 32.3 us -> 0 us
  starting transfers between devices: 0.36 us -> 22.2 us
    all_gather x9 -> x1, waiting for transfers between devices: 457 us -> 0.02 us  [local(): gain = lax.all_gather(smoother_gain.T, 'state', axis=0, tiled=True)]
    dot_general x131 -> x13, matrix products: 277 us -> 4.04 us  [high_dot(): jnp.dot(left, right, precision=lax.Precision.HIGH, preferred_element_type...]
    pallas_call x0 -> x6, Pallas kernels: none -> 81 us  [call(): pl.pallas_call(kernel, out_shape=outs, in_specs=specs, out_specs=jax.tree...]
    dynamic_slice x48 -> x1, local copies, waits for them, and re-layouts: 49.4 us -> 0.08 us  [local(): patterns = lax.dynamic_slice_in_dim(padded, quads * block, 8 * quads, 0)]
    while x131 -> x0, local copies, waits for them, and re-layouts: 39 us -> none  [the longest x1 33.5 us: prefix(): return lax.fori_loop(0, ahead, one, state)]
    all_gather x1 -> x0, local copies, waits for them, and re-layouts: 33.5 us -> none  [prefix(): gathered = jax.tree.map(lambda a: lax.all_gather(a, axis), part)]
    all_to_all x0 -> x2, blocking collectives: none -> 32.4 us  [the longest x1 19.2 us: local(): scan = lax.all_to_all(back, 'tm', 0, 0, tiled=True)]
    another operation x8 -> x0, loops' own time: 32.3 us -> none  [the longest x2 19.7 us: run_forward(): return lax.scan(advance, start, (drive, mask))[1]]
  transfers between devices with their start and end apart: 9 -> 19, of which waited for: 7 -> 9; matrix products, arithmetic and copies ran while one was open for 32% -> 3% of each run, Pallas kernels for 0% -> 1%
where the time goes in v1:
time: 201 us; the launch traced here: 200 us
  Pallas kernels  81 us (40%)
  waiting for transfers between devices  34 us (17%)
  blocking collectives  32.4 us (16%)
  starting transfers between devices  22.2 us (11%)
  between operations  14.6 us (7%)
  local copies, waits for them, and re-layouts  7.87 us (4%)
  matrix products  4.04 us (2%)
  other arithmetic  3.58 us (2%)
    pallas_call x6, Pallas kernels, call(): pl.pallas_call(kernel, out_shape=outs, in_specs=specs, out_specs=jax.tree...  81 us
    ppermute x8, waiting for transfers between devices, later(): moved = lax.ppermute(a, 'tm', [(i, (i + k) % count) for i in range(count)])  31.1 us
    all_to_all x1, blocking collectives, local(): scan = lax.all_to_all(back, 'tm', 0, 0, tiled=True)  19.2 us
    all_to_all x1, blocking collectives, local(): back_in = lax.all_to_all(ahead, 'tm', 0, 0, tiled=True)  13.1 us
    all_to_all x1, starting transfers between devices, local(): lax.all_to_all(jnp.tile(code[None], (count, 1)), 'tm', 0, 0, tiled=True)  11.5 us
    unnamed x23, local copies, waits for them, and re-layouts  5.65 us
    ppermute x3, starting transfers between devices, along_x(): lax.ppermute(a, 'state', [(2 * i + c, 2 * ((i + k) % chips) + c) for i in...  4.83 us
    ppermute x8, starting transfers between devices, later(): moved = lax.ppermute(a, 'tm', [(i, (i + k) % count) for i in range(count)])  4.63 us
  transfers between devices with their start and end apart: 19, of which 9 were waited for; matrix products, arithmetic and copies ran while one was open for 3% of the time, Pallas kernels for 1%

profile of v1, /device:TPU:2, one launch (start us, length us, event | category | flops | bytes accessed | tf_op | source)
XLA Modules:
  0.0 199.6 jit_solution(15374503355535344692)
XLA Ops:
  7.2 1.0 pad_maximum_fusion.refs_0_
  8.3 2.3 %collective-permute-start.2 = (f32[2,64,512]{2,1,0:T(8,128)S(1)}, f32[2,64,512]{2,1,0:T(8,128)S(1)}, u32[]{:S(2)}, u32[]{:S(2)}) collective-permute-start(f32[2,64,512]{2,1,0:T(8,128)S(1)} %pad_maximum_fusion.refs_0_), channel_id=1, source_target_pairs={{0,6},{1,7},{2,0},{3,1},{4,2},{5,3},{6,4},{7,5},{8,14},{9,15},{10,... | collective-permute-start | bytes 786440 | tf_op jit(solution)/shard_map/ppermute | solution.py:218
  10.6 0.7 collective-permute-start.1
  11.3 1.8 collective-permute-start
  13.1 0.7 reshape.38
  13.8 0.8 multiply_reduce_fusion
  15.2 11.5 %all-to-all-start = ((s32[32,1,4]{2,1,0:T(1,128)}), s32[32,1,4]{2,1,0:T(1,128)S(1)}, u32[]{:S(2)}, u32[]{:S(2)}) async-start(s32[32,1,4]{2,1,0:T(1,128)} %tile.2), calls=%async_computation | async-start | bytes 32768 | tf_op jit(solution)/shard_map/all_to_all | solution.py:238
  27.7 0.8 broadcast_select_fusion.4.refs_9_
  28.5 1.1 copy-done.1
  29.6 1.0 copy-done.2
  31.3 1.3 drive.1.refs_8_.drive_ref
  32.6 1.0 copy-done
  33.6 2.8 %all-to-all-done = s32[32,1,4]{2,1,0:T(1,128)S(1)} async-done(((s32[32,1,4]{2,1,0:T(1,128)}), s32[32,1,4]{2,1,0:T(1,128)S(1)}, u32[]{:S(2)}, u32[]{:S(2)}) %all-to-all-start) | async-done | bytes 544 | tf_op jit(solution)/shard_map/all_to_all | solution.py:238
  36.9 0.7 reduce.3
  38.4 7.2 %local.1 = (f32[32,512]{1,0:T(8,128)S(1)}, bf16[2,512,512]{2,1,0:T(8,128)(2,1)S(1)}, bf16[2,512,512]{2,1,0:T(8,128)(2,1)}) custom-call(s32[8]{0:T(128)S(1)} %pad_add_fusion.2.place_ref, s32[16]{0:T(128)S(1)} %copy-done.4, f32[2,64,512]{2,1,0:T(8,128)S(1)} %pad_maximum_fusion.refs_0_, f32[2,64,512]{2,1,0:T(8,128)S(1)} %collective-permute-done.refs_1_, ...), custom_call_target="tpu_custom_call" | custom-call | flops 2013265920 | bytes 4194304 | tf_op jit(solution)/shard_map/local/pallas_call | solution.py:34
  46.2 1.2 collective-permute-start.9
  47.5 1.5 collective-permute-start.8
  49.1 1.9 collective-permute-done.10
  51.0 1.6 collective-permute-done.9
  52.6 2.8 %collective-permute-done.8 = f32[32,512]{1,0:T(8,128)S(1)} collective-permute-done((f32[32,512]{1,0:T(8,128)S(1)}, f32[32,512]{1,0:T(8,128)S(1)}, u32[]{:S(2)}, u32[]{:S(2)}) %collective-permute-start.8) | collective-permute-done | bytes 65568 | tf_op jit(solution)/shard_map/ppermute | solution.py:226
  55.4 1.1 collective-permute-done.7
  56.5 1.2 copy-done.7
  57.7 46.1 %table.1 = (f32[32,512]{1,0:T(8,128)S(1)}, f32[512,256]{1,0:T(8,128)S(1)}, f32[512,256]{1,0:T(8,128)S(1)}) custom-call(s32[1]{0:T(128)} %bitcast.1.core_ref, s32[32]{0:T(128)S(1)} %pad_dynamic-slice_fusion.pattern_ref, bf16[2,512,512]{2,1,0:T(8,128)(2,1)S(1)} %get-tuple-element.20.high_ref.fh_ref.bh_ref, bf16[2,512,512]{2,1,0:T(8,128)(2,1)S(1)} %copy-done.7, ...), custom_call_target="tpu_custom_call" | custom-call | flops 16106127360 | bytes 4194304 | tf_op jit(solution)/shard_map/table/pallas_call | solution.py:34
  104.5 5.2 %collective-permute-done.11 = f32[32,512]{1,0:T(8,128)S(1)} collective-permute-done((f32[32,512]{1,0:T(8,128)S(1)}, f32[32,512]{1,0:T(8,128)S(1)}, u32[]{:S(2)}, u32[]{:S(2)}) %collective-permute-start.11) | collective-permute-done | bytes 65568 | tf_op jit(solution)/shard_map/ppermute | solution.py:226
  110.8 6.0 %collective-permute-done.13 = f32[32,512]{1,0:T(8,128)S(1)} collective-permute-done((f32[32,512]{1,0:T(8,128)S(1)}, f32[32,512]{1,0:T(8,128)S(1)}, u32[]{:S(2)}, u32[]{:S(2)}) %collective-permute-start.13) | collective-permute-done | bytes 65568 | tf_op jit(solution)/shard_map/ppermute | solution.py:226
  117.5 6.2 %collective-permute-done.15 = f32[32,512]{1,0:T(8,128)S(1)} collective-permute-done((f32[32,512]{1,0:T(8,128)S(1)}, f32[32,512]{1,0:T(8,128)S(1)}, u32[]{:S(2)}, u32[]{:S(2)}) %collective-permute-start.15) | collective-permute-done | bytes 65568 | tf_op jit(solution)/shard_map/ppermute | solution.py:226
  124.5 6.4 %collective-permute-done.16 = f32[32,512]{1,0:T(8,128)S(1)} collective-permute-done((f32[32,512]{1,0:T(8,128)S(1)}, f32[32,512]{1,0:T(8,128)S(1)}, u32[]{:S(2)}, u32[]{:S(2)}) %collective-permute-start.16) | collective-permute-done | bytes 65568 | tf_op jit(solution)/shard_map/ppermute | solution.py:226
  131.5 13.7 %powers.1 = (bf16[512,512]{1,0:T(8,128)(2,1)S(1)}, bf16[512,512]{1,0:T(8,128)(2,1)S(1)}, bf16[512,512]{1,0:T(8,128)(2,1)S(1)}, bf16[512,512]{1,0:T(8,128)(2,1)S(...) custom-call(f32[512,512]{1,0:T(8,128)} %all-gather.2.cloned.1.call-done.gain_ref, ...), custom_call_target="tpu_custom_call" | custom-call | flops 7247757312 | bytes 4194304 | tf_op jit(solution)/shard_map/powers/pallas_call | solution.py:34
  145.1 9.7 %forward.1 = (f32[16,32,512]{2,1,0:T(8,128)}, f32[4,4,32,512]{3,2,1,0:T(8,128)}, f32[4,32,512]{2,1,0:T(8,128)S(1)}, f32[32,512]{1,0:T(8,128)S(1)}, f32[32,512]{1,0:T(8,128)S(1)}) custom-call(s32[16]{0:T(128)S(1)} %copy-done.5, s32[1]{0:T(128)} %bitcast.final_ref, f32[32,512]{1,0:T(8,128)S(1)} %fusion.16.start_ref, f32[16,32,512]{2,1,0:T(8,128)} %copy-done, ...), custom_call_target="tpu_custom_call" | custom-call | flops 2013265920 | bytes 4194304 | tf_op jit(solution)/shard_map/forward/pallas_call | solution.py:34
  155.0 19.2 %all_to_all.30 = f32[32,1,512]{2,1,0:T(1,128)S(1)} all-to-all(f32[32,1,512]{2,1,0:T(1,128)S(1)} %copy.10), channel_id=1, replica_groups=mesh['tm'=32,'state'=8] {'tm'}, dimensions={0} | all-to-all | bytes 131072 | tf_op jit(solution)/shard_map/all_to_all | solution.py:318
  176.5 13.1 %all_to_all.31 = f32[32,1,512]{2,1,0:T(1,128)S(1)} all-to-all(f32[32,1,512]{2,1,0:T(1,128)S(1)} %copy.12), channel_id=1, replica_groups=mesh['tm'=32,'state'=8] {'tm'}, dimensions={0} | all-to-all | bytes 131072 | tf_op jit(solution)/shard_map/all_to_all | solution.py:323
  189.7 3.1 %backward.1 = f32[4,4,32,512]{3,2,1,0:T(8,128)} custom-call(f32[32,512]{1,0:T(8,128)S(1)} %bitcast_select_fusion.start_ref, f32[4,4,32,512]{3,2,1,0:T(8,128)S(1)} %copy-done.8, f32[4,32,512]{2,1,0:T(8,128)S(1)} %get-tuple-element.37.part_ref, bf16[512,512]{1,0:T(8,128)(2,1)S(1)} %get-tuple-element.26.gh_ref, bf16[512,512]{1,0:T(8,128)(2,1)S(1)} %get-tuple-element.27.gl_ref, ...), custom_call_target="tpu_custom_call" | custom-call | flops 2013265920 | bytes 4194304 | tf_op jit(solution)/shard_map/backward/pallas_call | solution.py:34
  (81 shorter events, 10.4 us)
Async XLA Ops:
  8.2 29.5 %collective-permute-start.3 = (f32[2,64,512]{2,1,0:T(8,128)S(1)}, f32[2,64,512]{2,1,0:T(8,128)S(1)}, u32[]{:S(2)}, u32[]{:S(2)}) collective-permute-start(f32[2,64,512]{2,1,0:T(8,128)S(1)} %pad_maximum_fusion.refs_0_), channel_id=1, source_target_pairs={{0,1},{1,0},{2,3},{3,2},{4,5},{5,4},{6,7},{7,6},{8,9},{9,8},{10,11... | collective-permute-start | bytes 786440 | tf_op jit(solution)/shard_map/ppermute | solution.py:223
  8.3 18.8 %collective-permute-start.2 = (f32[2,64,512]{2,1,0:T(8,128)S(1)}, f32[2,64,512]{2,1,0:T(8,128)S(1)}, u32[]{:S(2)}, u32[]{:S(2)}) collective-permute-start(f32[2,64,512]{2,1,0:T(8,128)S(1)} %pad_maximum_fusion.refs_0_), channel_id=1, source_target_pairs={{0,6},{1,7},{2,0},{3,1},{4,2},{5,3},{6,4},{7,5},{8,14},{9,15},{10,... | collective-permute-start | bytes 786440 | tf_op jit(solution)/shard_map/ppermute | solution.py:218
  10.6 16.5 %collective-permute-start.1 = (f32[2,64,512]{2,1,0:T(8,128)S(1)}, f32[2,64,512]{2,1,0:T(8,128)S(1)}, u32[]{:S(2)}, u32[]{:S(2)}) collective-permute-start(f32[2,64,512]{2,1,0:T(8,128)S(1)} %pad_maximum_fusion.refs_0_), channel_id=1, source_target_pairs={{0,4},{1,5},{2,6},{3,7},{4,0},{5,1},{6,2},{7,3},{8,12},{9,13},{10,... | collective-permute-start | bytes 786440 | tf_op jit(solution)/shard_map/ppermute | solution.py:218
  11.3 16.3 %collective-permute-start = (f32[2,64,512]{2,1,0:T(8,128)S(1)}, f32[2,64,512]{2,1,0:T(8,128)S(1)}, u32[]{:S(2)}, u32[]{:S(2)}) collective-permute-start(f32[2,64,512]{2,1,0:T(8,128)S(1)} %pad_maximum_fusion.refs_0_), channel_id=1, source_target_pairs={{0,2},{1,3},{2,4},{3,5},{4,6},{5,7},{6,0},{7,1},{8,10},{9,11},{10,... | collective-permute-start | bytes 786440 | tf_op jit(solution)/shard_map/ppermute | solution.py:218
  15.2 21.2 %all-to-all-start = ((s32[32,1,4]{2,1,0:T(1,128)}), s32[32,1,4]{2,1,0:T(1,128)S(1)}, u32[]{:S(2)}, u32[]{:S(2)}) async-start(s32[32,1,4]{2,1,0:T(1,128)} %tile.2), calls=%async_computation | async-start | bytes 32768 | tf_op jit(solution)/shard_map/all_to_all | solution.py:238
  26.7 104.8 %all-gather.2.cloned.1.call-start = ((), (), s32[]{:S(2)}) async-start(), calls=%async_computation.3 | async-start | bytes 1179648 | tf_op jit(solution)/shard_map/all_gather | solution.py:234
  27.0 10.7 %collective-permute-start.6 = (f32[2,64,512]{2,1,0:T(8,128)S(1)}, f32[2,64,512]{2,1,0:T(8,128)S(1)}, u32[]{:S(2)}, u32[]{:S(2)}) collective-permute-start(f32[2,64,512]{2,1,0:T(8,128)S(1)} %collective-permute-done.2.refs_3_), channel_id=1, source_target_pairs={{0,1},{1,0},{2,3},{3,2},{4,5},{5,4},{6,7},{7,6},{8,9},{9,8},{10,11... | collective-permute-start | bytes 786440 | tf_op jit(solution)/shard_map/ppermute | solution.py:223
  27.1 10.6 %collective-permute-start.5 = (f32[2,64,512]{2,1,0:T(8,128)S(1)}, f32[2,64,512]{2,1,0:T(8,128)S(1)}, u32[]{:S(2)}, u32[]{:S(2)}) collective-permute-start(f32[2,64,512]{2,1,0:T(8,128)S(1)} %collective-permute-done.1.refs_2_), channel_id=1, source_target_pairs={{0,1},{1,0},{2,3},{3,2},{4,5},{5,4},{6,7},{7,6},{8,9},{9,8},{10,11... | collective-permute-start | bytes 786440 | tf_op jit(solution)/shard_map/ppermute | solution.py:223
  27.6 10.2 %collective-permute-start.4 = (f32[2,64,512]{2,1,0:T(8,128)S(1)}, f32[2,64,512]{2,1,0:T(8,128)S(1)}, u32[]{:S(2)}, u32[]{:S(2)}) collective-permute-start(f32[2,64,512]{2,1,0:T(8,128)S(1)} %collective-permute-done.refs_1_), channel_id=1, source_target_pairs={{0,1},{1,0},{2,3},{3,2},{4,5},{5,4},{6,7},{7,6},{8,9},{9,8},{10,11... | collective-permute-start | bytes 786440 | tf_op jit(solution)/shard_map/ppermute | solution.py:223
  28.5 1.1 copy-start.1
  29.6 1.0 copy-start.2
  30.6 0.7 copy-start.3
  32.6 1.0 copy-start
  37.7 0.7 copy-start.4
  45.5 58.3 %copy-start.6 = (bf16[2,512,512]{2,1,0:T(8,128)(2,1)}, bf16[2,512,512]{2,1,0:T(8,128)(2,1)S(1)}, u32[]{:S(2)}) copy-start(bf16[2,512,512]{2,1,0:T(8,128)(2,1)S(1)} %get-tuple-element.20.high_ref.fh_ref.bh_ref) | copy-start | bytes 3145732
  45.5 5.5 %collective-permute-start.10 = (f32[32,512]{1,0:T(8,128)S(1)}, f32[32,512]{1,0:T(8,128)S(1)}, u32[]{:S(2)}, u32[]{:S(2)}) collective-permute-start(f32[32,512]{1,0:T(8,128)S(1)} %get-tuple-element.22), channel_id=1, source_target_pairs={{0,32},{8,40},{16,48},{24,56},{32,64},{40,72},{48,80},{56,88},{64,... | collective-permute-start | bytes 196616 | tf_op jit(solution)/shard_map/ppermute | solution.py:226
  46.2 6.4 %collective-permute-start.9 = (f32[32,512]{1,0:T(8,128)S(1)}, f32[32,512]{1,0:T(8,128)S(1)}, u32[]{:S(2)}, u32[]{:S(2)}) collective-permute-start(f32[32,512]{1,0:T(8,128)S(1)} %get-tuple-element.22), channel_id=1, source_target_pairs={{0,24},{8,32},{16,40},{24,48},{32,56},{40,64},{48,72},{56,80},{64,... | collective-permute-start | bytes 196616 | tf_op jit(solution)/shard_map/ppermute | solution.py:226
  47.5 8.0 %collective-permute-start.8 = (f32[32,512]{1,0:T(8,128)S(1)}, f32[32,512]{1,0:T(8,128)S(1)}, u32[]{:S(2)}, u32[]{:S(2)}) collective-permute-start(f32[32,512]{1,0:T(8,128)S(1)} %get-tuple-element.22), channel_id=1, source_target_pairs={{0,16},{8,24},{16,32},{24,40},{32,48},{40,56},{48,64},{56,72},{64,... | collective-permute-start | bytes 196616 | tf_op jit(solution)/shard_map/ppermute | solution.py:226
  48.9 7.6 %collective-permute-start.7 = (f32[32,512]{1,0:T(8,128)S(1)}, f32[32,512]{1,0:T(8,128)S(1)}, u32[]{:S(2)}, u32[]{:S(2)}) collective-permute-start(f32[32,512]{1,0:T(8,128)S(1)} %get-tuple-element.22), channel_id=1, source_target_pairs={{0,8},{8,16},{16,24},{24,32},{32,40},{40,48},{48,56},{56,64},{64,7... | collective-permute-start | bytes 196616 | tf_op jit(solution)/shard_map/ppermute | solution.py:226
  56.5 1.2 copy-start.7
  103.8 27.6 %copy-start.10 = (f32[32,512]{1,0:T(8,128)S(1)}, f32[32,512]{1,0:T(8,128)}, u32[]{:S(2)}) copy-start(f32[32,512]{1,0:T(8,128)} %param.14) | copy-start | bytes 196612
  103.9 6.1 %collective-permute-start.12 = (f32[512,256]{1,0:T(8,128)S(1)}, f32[512,256]{1,0:T(8,128)S(1)}, u32[]{:S(2)}, u32[]{:S(2)}) collective-permute-start(f32[512,256]{1,0:T(8,128)S(1)} %get-tuple-element.24), channel_id=1, source_target_pairs={{0,1},{1,0},{2,3},{3,2},{4,5},{5,4},{6,7},{7,6},{8,9},{9,8},{10,11... | collective-permute-start | bytes 1572872 | tf_op jit(solution)/shard_map/ppermute | solution.py:223
  104.0 5.7 %collective-permute-start.11 = (f32[32,512]{1,0:T(8,128)S(1)}, f32[32,512]{1,0:T(8,128)S(1)}, u32[]{:S(2)}, u32[]{:S(2)}) collective-permute-start(f32[32,512]{1,0:T(8,128)S(1)} %get-tuple-element.23), channel_id=1, source_target_pairs={{0,32},{8,40},{16,48},{24,56},{32,64},{40,72},{48,80},{56,88},{64,... | collective-permute-start | bytes 196616 | tf_op jit(solution)/shard_map/ppermute | solution.py:226
  104.1 12.9 %collective-permute-start.14 = (f32[512,256]{1,0:T(8,128)S(1)}, f32[512,256]{1,0:T(8,128)S(1)}, u32[]{:S(2)}, u32[]{:S(2)}) collective-permute-start(f32[512,256]{1,0:T(8,128)S(1)} %get-tuple-element.25), channel_id=1, source_target_pairs={{0,1},{1,0},{2,3},{3,2},{4,5},{5,4},{6,7},{7,6},{8,9},{9,8},{10,11... | collective-permute-start | bytes 1572872 | tf_op jit(solution)/shard_map/ppermute | solution.py:223
  110.2 6.5 %collective-permute-start.13 = (f32[32,512]{1,0:T(8,128)S(1)}, f32[32,512]{1,0:T(8,128)S(1)}, u32[]{:S(2)}, u32[]{:S(2)}) collective-permute-start(f32[32,512]{1,0:T(8,128)S(1)} %fusion.12), channel_id=1, source_target_pairs={{0,64},{8,72},{16,80},{24,88},{32,96},{40,104},{48,112},{56,120},{... | collective-permute-start | bytes 196616 | tf_op jit(solution)/shard_map/ppermute | solution.py:226
  117.3 6.5 %collective-permute-start.15 = (f32[32,512]{1,0:T(8,128)S(1)}, f32[32,512]{1,0:T(8,128)S(1)}, u32[]{:S(2)}, u32[]{:S(2)}) collective-permute-start(f32[32,512]{1,0:T(8,128)S(1)} %fusion.13), channel_id=1, source_target_pairs={{0,64},{8,72},{16,80},{24,88},{32,96},{40,104},{48,112},{56,120},{... | collective-permute-start | bytes 196616 | tf_op jit(solution)/shard_map/ppermute | solution.py:226
  124.2 6.7 %collective-permute-start.16 = (f32[32,512]{1,0:T(8,128)S(1)}, f32[32,512]{1,0:T(8,128)S(1)}, u32[]{:S(2)}, u32[]{:S(2)}) collective-permute-start(f32[32,512]{1,0:T(8,128)S(1)} %fusion.14), channel_id=1, source_target_pairs={{0,64},{8,72},{16,80},{24,88},{32,96},{40,104},{48,112},{56,120},{... | collective-permute-start | bytes 196616 | tf_op jit(solution)/shard_map/ppermute | solution.py:226
  131.4 13.7 %copy-start.5 = (s32[16]{0:T(128)S(1)}, s32[16]{0:T(128)}, u32[]{:S(2)}) copy-start(s32[16]{0:T(128)} %mask_ref.5) | copy-start | bytes 196
  145.1 29.1 %copy-start.9 = (f32[5,512,512]{2,1,0:T(8,128)S(1)}, f32[5,512,512]{2,1,0:T(8,128)}, u32[]{:S(2)}) copy-start(f32[5,512,512]{2,1,0:T(8,128)} %get-tuple-element.35) | copy-start | bytes 15728644
  154.9 34.8 %copy-start.8 = (f32[4,4,32,512]{3,2,1,0:T(8,128)S(1)}, f32[4,4,32,512]{3,2,1,0:T(8,128)}, u32[]{:S(2)}) copy-start(f32[4,4,32,512]{3,2,1,0:T(8,128)} %get-tuple-element.36.gap_ref) | copy-start | bytes 3145732
Sparse Core Ops, SparseCore 0:
  110.9 20.1 all-gather.1
